TPU v7x, 256 devices: a whole 4x4x8 slice. The times are simulated.
256 devices in a mesh: seq: 64 (over y_hi, x, z), chan: 4 (over y_lo, core).
Axes of the slice: x: 4, y: 4 (y_hi: 2, y_lo: 2; y = y_hi * 2 + y_lo), z: 8, core: 2. Of those that a mesh axis runs over, the one named last changes fastest.
Arguments:
- inputs: bfloat16 [16384, 2048], P('seq', 'chan'), may hold values from -6 to 6
- weights: bfloat16 [4, 2048, 2048], P(None, None, 'chan'), may hold values from -0.125 to 0.125
- filters: float32 [4, 16384], P(None, 'seq'), may hold values from -0.046875 to 0.046875
Outputs:
- output: bfloat16 [16384, 2048], P('seq', 'chan')
All inputs are finite; a program needn't handle non-finite values.
Results may differ from a plain program's by a relative error of at most 0.0049.
Values may be sent and summed in bfloat16 or wider, within the bound.
A program may use at most 64 MiB of HBM per device.

v0:
```python
import functools

import jax
import jax.numpy as jnp
from jax import lax
from jax.experimental import pallas as pl
from jax.experimental.pallas import tpu as pltpu
from jax.sharding import PartitionSpec as P

MESH = pl.DeviceIdType.MESH
SEQ = 64
CHAN = 4
K = 4
TOK = 256
FEAT = 512
HALF = 128
SHARE = FEAT // SEQ
LAGS = 8
PARTS = 4


def peer(s, o):
    yh, x, z = s // 32, (s // 8) % 4, s % 8
    oy, ox, oz = o // 32, o % 4, (o // 4) % 8
    return ((yh + oy) % 2) * 32 + ((x + ox) % 4) * 8 + (z + oz) % 8


def wait_bytes(ref, sem):
    pltpu.make_async_copy(ref, ref, sem).wait()


def toeplitz(flt, table):
    row = lax.broadcasted_iota(jnp.int32, (HALF, HALF), 0)
    col = lax.broadcasted_iota(jnp.int32, (HALF, HALF), 1)
    same = col >= row

    def turned(line):
        return pltpu.roll(
            jnp.broadcast_to(line, (HALF, HALF)), 0, axis=1, stride=1, stride_axis=0
        )

    for k in range(K):
        table[k, 0] = jnp.zeros((HALF, HALF), jnp.bfloat16)

        def step(m, before):
            first = turned(flt[m, pl.ds(k, 1), :])
            table[k, 2 * m + 1] = jnp.where(same, first, before).astype(jnp.bfloat16)
            second = turned(flt[m, pl.ds(K + k, 1), :])
            table[k, 2 * m + 2] = jnp.where(same, second, first).astype(jnp.bfloat16)
            return second

        lax.fori_loop(0, SEQ, step, jnp.zeros((HALF, HALF), jnp.float32))


def load_blocks(got, k, even, odd):
    v = got[k].astype(jnp.float32)
    a = jnp.concatenate([v[:, :SHARE, :], v[:, SHARE:, :]], axis=2)
    a = a.reshape(SEQ * SHARE, TOK)
    even[pl.ds(64, 512), :] = a.astype(jnp.bfloat16)
    zero = jnp.zeros((SHARE, TOK), jnp.float32)
    odd[pl.ds(64, 528), :] = jnp.concatenate([zero, a, zero], axis=0).astype(jnp.bfloat16)


def conv_lags(table, even, odd, acc, k, group, fresh):
    low = 64 * group
    rows = 512 - low
    lhs, rhs = [], []
    for jj in range(LAGS):
        at = 64 - 8 * jj
        lhs.append(even[at : at + rows, :] if jj % 2 == 0 else odd[at + 8 : at + 8 + rows, :])
        n = 2 * (LAGS * group + jj) + 1
        rhs.append(jnp.concatenate([table[k, n], table[k, n + 1]], axis=1))
        rhs.append(jnp.concatenate([table[k, n - 1], table[k, n]], axis=1))
    part = jnp.dot(
        jnp.concatenate(lhs, axis=1),
        jnp.concatenate(rhs, axis=0),
        preferred_element_type=jnp.float32,
    )
    if fresh:
        acc[low:, :] = part
    else:
        acc[low:, :] += part


def kernel(
    x_ref, w_hbm, f_ref, o_ref,
    xs, w, fsrc, flt, out_p, got, table, even, odd, acc, out_y, got_y,
    w_sem, xs_send, xs_recv, f_send, f_recv, p_send, p_recv, y_send, y_recv,
):
    s, c = lax.axis_index("seq"), lax.axis_index("chan")
    mate = c + 1 - 2 * (c % 2)
    across = (c + 2) % 4

    bar = pltpu.get_barrier_semaphore()
    for i in range(1, CHAN):
        pl.semaphore_signal(bar, inc=1, device_id=(s, (c + i) % CHAN), device_id_type=MESH)

    @pl.loop(1, SEQ)
    def _(o):
        pl.semaphore_signal(bar, inc=1, device_id=(peer(s, o), c), device_id_type=MESH)

    for k in range(K):
        pltpu.make_async_copy(w_hbm.at[k], w.at[k], w_sem.at[k]).start()
    f = f_ref[...]
    fsrc[...] = jnp.concatenate([f[:, :HALF], f[:, HALF:]], axis=0)
    xs[pl.ds(c, 1)] = x_ref[...][None]
    flt[pl.ds(s, 1)] = fsrc[...][None]
    even[0:64, :] = jnp.zeros((64, TOK), jnp.bfloat16)
    odd[0:64, :] = jnp.zeros((64, TOK), jnp.bfloat16)
    pl.semaphore_wait(bar, SEQ - 1 + CHAN - 1)

    rows = TOK // PARTS

    def x_copy(owner, part, to, kind):
        at = xs.at[owner, pl.ds(part * rows, rows)]
        return pltpu.make_async_remote_copy(
            at, at, xs_send.at[kind, part], xs_recv.at[kind, part],
            device_id=(s, to), device_id_type=MESH,
        )

    for part in range(PARTS):
        x_copy(c, part, across, 0).start()
    for part in range(PARTS):
        x_copy(c, part, mate, 1).start()

    @pl.loop(1, SEQ)
    def _(o):
        pltpu.make_async_remote_copy(
            fsrc, flt.at[s], f_send, f_recv, device_id=(peer(s, o), c), device_id_type=MESH
        ).start()

    for part in range(PARTS):
        x_copy(across, part, across, 0).wait_recv()
        x_copy(across, part, mate, 2).start()
    for part in range(PARTS):
        x_copy(mate, part, mate, 1).wait_recv()
    for part in range(PARTS):
        x_copy((across + mate - c + 4) % 4, part, mate, 2).wait_recv()

    for k in range(K):
        pltpu.make_async_copy(w_hbm.at[k], w.at[k], w_sem.at[k]).wait()
        p = None
        for i in range(CHAN):
            d = jnp.dot(
                xs[i], w[k, i * FEAT : (i + 1) * FEAT, :], preferred_element_type=jnp.float32
            )
            p = d if p is None else p + d
        t = p.T.reshape(SEQ, SHARE, TOK)
        out_p[k] = jnp.concatenate([t[:, :, :HALF], t[:, :, HALF:]], axis=1).astype(jnp.bfloat16)

        @pl.loop(1, SEQ)
        def _(o):
            to = peer(s, o)
            pltpu.make_async_remote_copy(
                out_p.at[k, to], got.at[k, s], p_send.at[k], p_recv.at[k],
                device_id=(to, c), device_id_type=MESH,
            ).start()

        got[k, pl.ds(s, 1)] = out_p[k, pl.ds(s, 1)]

    wait_bytes(flt.at[pl.ds(0, SEQ - 1)], f_recv)
    toeplitz(flt, table)

    for k in range(K):
        wait_bytes(got.at[k, pl.ds(0, SEQ - 1)], p_recv.at[k])
        load_blocks(got, k, even, odd)
        for group in range(SEQ // LAGS):
            conv_lags(table, even, odd, acc, k, group, k == 0 and group == 0)

    y = acc[...].reshape(SEQ, SHARE, TOK)
    out_y[...] = jnp.concatenate([y[:, :, :HALF], y[:, :, HALF:]], axis=1).astype(jnp.bfloat16)

    @pl.loop(1, SEQ)
    def _(o):
        to = peer(s, o)
        pltpu.make_async_remote_copy(
            out_y.at[to], got_y.at[s], y_send, y_recv, device_id=(to, c), device_id_type=MESH
        ).start()

    got_y[pl.ds(s, 1)] = out_y[pl.ds(s, 1)]
    for part in range(PARTS):
        x_copy(c, part, across, 0).wait_send()
        x_copy(c, part, mate, 1).wait_send()
        x_copy(across, part, mate, 2).wait_send()
    wait_bytes(flt.at[pl.ds(0, SEQ - 1)], f_send)
    for k in range(K):
        wait_bytes(out_p.at[k, pl.ds(0, SEQ - 1)], p_send.at[k])

    wait_bytes(got_y.at[pl.ds(0, SEQ - 1)], y_recv)
    r = got_y[...].astype(jnp.float32)
    for half in range(2):
        block = r[:, half * SHARE : (half + 1) * SHARE, :].reshape(FEAT, HALF)
        o_ref[half * HALF : (half + 1) * HALF, :] = block.T.astype(jnp.bfloat16)
    wait_bytes(out_y.at[pl.ds(0, SEQ - 1)], y_send)


def local(inputs, weights, filters):
    bf16, f32 = jnp.bfloat16, jnp.float32
    vmem = pl.BlockSpec(memory_space=pltpu.VMEM)
    dma = pltpu.SemaphoreType.DMA
    return pl.pallas_call(
        kernel,
        out_shape=jax.ShapeDtypeStruct((TOK, FEAT), bf16),
        in_specs=[vmem, pl.BlockSpec(memory_space=pl.ANY), vmem],
        out_specs=vmem,
        scratch_shapes=[
            pltpu.VMEM((CHAN, TOK, FEAT), bf16),
            pltpu.VMEM((K, CHAN * FEAT, FEAT), bf16),
            pltpu.VMEM((8, HALF), f32),
            pltpu.VMEM((SEQ, 8, HALF), f32),
            pltpu.VMEM((K, SEQ, 16, HALF), bf16),
            pltpu.VMEM((K, SEQ, 16, HALF), bf16),
            pltpu.VMEM((K, 2 * SEQ + 1, HALF, HALF), bf16),
            pltpu.VMEM((576, TOK), bf16),
            pltpu.VMEM((592, TOK), bf16),
            pltpu.VMEM((512, TOK), f32),
            pltpu.VMEM((SEQ, 16, HALF), bf16),
            pltpu.VMEM((SEQ, 16, HALF), bf16),
            dma((K,)),
            dma((3, PARTS)),
            dma((3, PARTS)),
            dma,
            dma,
            dma((K,)),
            dma((K,)),
            dma,
            dma,
        ],
        compiler_params=pltpu.CompilerParams(
            collective_id=0, has_side_effects=True, vmem_limit_bytes=56 << 20
        ),
        cost_estimate=pl.CostEstimate(
            flops=11 * 10**9, bytes_accessed=10**7, transcendentals=0
        ),
    )(inputs, weights, filters)


def solution(mesh):
    in_specs = (P("seq", "chan"), P(None, None, "chan"), P(None, "seq"))
    out_specs = P("seq", "chan")
    return jax.shard_map(local, mesh=mesh, in_specs=in_specs, out_specs=out_specs, check_vma=False)
```

profile of v0, /device:TPU:1, one launch (start us, length us, event | category | flops | bytes accessed | tf_op | source)
XLA Modules:
  0.0 87.6 jit_solution(13095731818037610519)
XLA Ops:
  0.0 85.9 %shard_map.37 = bf16[256,512]{1,0:T(8,128)(2,1)} custom-call(bf16[256,512]{1,0:T(8,128)(2,1)} %x_ref.1, bf16[4,2048,512]{2,1,0:T(8,128)(2,1)} %w_hbm.1, f32[4,256]{1,0:T(4,128)} %f_ref.1), custom_call_target="tpu_custom_call" | custom-call | flops 11000000512 | bytes 10000000 | tf_op jit(solution)/shard_map/pallas_call | solution.py:201
  85.9 1.7 %copy.5 = bf16[256,512]{1,0:T(8,128)(2,1)} copy(bf16[256,512]{1,0:T(8,128)(2,1)} %shard_map.37) | data formatting | bytes 524288
where the time goes:
time: 87.7 us; the launch traced here: 87.6 us
  Pallas kernels  85.9 us (98%)
  local copies, waits for them, and re-layouts  1.67 us (2%)
    pallas_call x1, Pallas kernels, local(): pl.pallas_call(kernel, out_shape=jax.ShapeDtypeStruct((TOK, FEAT), bf16),...  85.9 us

commit v1 on v0

v1 whole, which is shorter than its diff:
```python
import functools

import jax
import jax.numpy as jnp
from jax import lax
from jax.experimental import pallas as pl
from jax.experimental.pallas import tpu as pltpu
from jax.sharding import PartitionSpec as P

MESH = pl.DeviceIdType.MESH
SEQ = 64
CHAN = 4
K = 4
TOK = 256
FEAT = 512
HALF = 128
SHARE = FEAT // SEQ
LAGS = 8
BLOCKS = 8
PARTS = 4


def peer(s, c, o):
    i, r = (SEQ - o) // 8, (SEQ - o) % 8
    h = (i + 1) // 2
    oz = h + (1 - i % 2) * (8 - 2 * h)
    oz = oz + (c % 2) * (8 - 2 * oz)
    yh, x, z = s // 32, (s // 8) % 4, s % 8
    return ((yh + r // 4) % 2) * 32 + ((x + r) % 4) * 8 + (z + oz) % 8


def wait_bytes(ref, sem):
    pltpu.make_async_copy(ref, ref, sem).wait()


def toeplitz(flt, table):
    row = lax.broadcasted_iota(jnp.int32, (16, HALF), 0)
    col = lax.broadcasted_iota(jnp.int32, (16, HALF), 1)

    def turned(line):
        wide = jnp.broadcast_to(line, (16, HALF))
        return pltpu.roll(wide, 0, axis=1, stride=1, stride_axis=0).astype(jnp.bfloat16)

    for k in range(K):
        table[k, 0] = jnp.zeros((HALF, HALF), jnp.bfloat16)

    def step(m0, carry):
        for k in range(K):
            last = flt[jnp.maximum(m0 * BLOCKS - 1, 0), pl.ds(K + k, 1), :]
            base = [turned(jnp.where(m0 == 0, 0.0, last))]
            for m in range(BLOCKS):
                for q in range(2):
                    base.append(turned(flt[m0 * BLOCKS + m, pl.ds(q * K + k, 1), :]))
            for i in range(HALF // 16):
                moved = base if i == 0 else [pltpu.roll(b, 16 * i, axis=1) for b in base]
                for n in range(2 * BLOCKS):
                    table[k, 2 * BLOCKS * m0 + n + 1, 16 * i : 16 * (i + 1), :] = jnp.where(
                        col >= row + 16 * i, moved[n + 1], moved[n]
                    )
        return carry

    lax.fori_loop(0, SEQ // BLOCKS, step, 0)


def load_blocks(got, chunk, even, odd):
    v = got[chunk].astype(jnp.float32)
    zero = jnp.zeros((SHARE, HALF), jnp.float32)
    for kk in range(2):
        a = v[:, kk * SHARE : (kk + 1) * SHARE, :].reshape(SEQ * SHARE, HALF)
        even[kk, 64:576, :] = a.astype(jnp.bfloat16)
        odd[kk, 64:592, :] = jnp.concatenate([zero, a, zero], axis=0).astype(jnp.bfloat16)


def conv_lags(table, even, odd, acc, chunk, group):
    half, pair = chunk // 2, chunk % 2
    low = 64 * group
    rows = 512 - low
    lhs, rhs = [], []
    for kk in range(2):
        for jj in range(LAGS):
            at = 64 - 8 * jj
            if jj % 2 == 0:
                lhs.append(even[kk, at : at + rows, :])
            else:
                lhs.append(odd[kk, at + 8 : at + 8 + rows, :])
            n = 2 * (LAGS * group + jj) + 1 - half
            k = 2 * pair + kk
            rhs.append(jnp.concatenate([table[k, n], table[k, n + 1]], axis=1))
    part = jnp.dot(
        jnp.concatenate(lhs, axis=1),
        jnp.concatenate(rhs, axis=0),
        preferred_element_type=jnp.float32,
    )
    if chunk == 0 and group == 0:
        acc[low:, :] = part
    else:
        acc[low:, :] += part


def kernel(
    x_ref, w_hbm, f_ref, o_ref,
    xs, w, fsrc, flt, part_p, out_p, got, table, even, odd, acc, out_y, got_y,
    w_sem, xs_send, xs_recv, f_send, f_recv, p_send, p_recv, y_send, y_recv,
):
    s, c = lax.axis_index("seq"), lax.axis_index("chan")
    mate = c + 1 - 2 * (c % 2)
    across = (c + 2) % 4
    diag = (mate + 2) % 4

    bar = pltpu.get_barrier_semaphore()
    for i in range(1, CHAN):
        pl.semaphore_signal(bar, inc=1, device_id=(s, (c + i) % CHAN), device_id_type=MESH)

    @pl.loop(1, SEQ)
    def _(o):
        pl.semaphore_signal(bar, inc=1, device_id=(peer(s, c, o), c), device_id_type=MESH)

    for k in range(K):
        pltpu.make_async_copy(w_hbm.at[k], w.at[k], w_sem.at[k]).start()
    f = f_ref[...]
    fsrc[...] = jnp.concatenate([f[:, :HALF], f[:, HALF:]], axis=0)
    xs[pl.ds(c, 1)] = x_ref[...][None]
    flt[pl.ds(s, 1)] = fsrc[...][None]
    for kk in range(2):
        even[kk, 0:64, :] = jnp.zeros((64, HALF), jnp.bfloat16)
        odd[kk, 0:64, :] = jnp.zeros((64, HALF), jnp.bfloat16)
    pl.semaphore_wait(bar, SEQ - 1 + CHAN - 1)

    rows = TOK // PARTS

    def x_copy(owner, part, to, kind):
        at = xs.at[owner, pl.ds(part * rows, rows)]
        return pltpu.make_async_remote_copy(
            at, at, xs_send.at[kind, part], xs_recv.at[kind, part],
            device_id=(s, to), device_id_type=MESH,
        )

    for part in range(PARTS):
        x_copy(c, part, across, 0).start()
    for part in range(PARTS):
        x_copy(c, part, mate, 1).start()

    @pl.loop(1, SEQ)
    def _(o):
        pltpu.make_async_remote_copy(
            fsrc, flt.at[s], f_send, f_recv, device_id=(peer(s, c, o), c), device_id_type=MESH
        ).start()

    def pass_on(part):
        x_copy(across, part, across, 0).wait_recv()
        x_copy(across, part, mate, 2).start()

    def project(owner, k, low, high):
        return jnp.dot(
            xs[owner, low:high, :],
            w[k, pl.ds(pl.multiple_of(owner * FEAT, FEAT), FEAT), :],
            preferred_element_type=jnp.float32,
        )

    for k in range(K):
        pltpu.make_async_copy(w_hbm.at[k], w.at[k], w_sem.at[k]).wait()
        part_p[k] = project(c, k, 0, TOK)
    pass_on(0)
    for part in range(PARTS):
        x_copy(mate, part, mate, 1).wait_recv()
    pass_on(1)
    for k in range(K):
        part_p[k] += project(mate, k, 0, TOK)

    for chunk in range(4):
        half, pair = chunk // 2, chunk % 2
        if chunk == 1:
            pass_on(2)
            pass_on(3)
        if pair == 0:
            x_copy(diag, 2 * half, mate, 2).wait_recv()
            x_copy(diag, 2 * half + 1, mate, 2).wait_recv()
        low, high = half * HALF, (half + 1) * HALF
        turned = []
        for k in (2 * pair, 2 * pair + 1):
            p = part_p[k, low:high, :] + project(across, k, low, high) + project(diag, k, low, high)
            turned.append(p.T.reshape(SEQ, SHARE, HALF))
        out_p[chunk] = jnp.concatenate(turned, axis=1).astype(jnp.bfloat16)

        @pl.loop(1, SEQ)
        def _(o):
            to = peer(s, c, o)
            pltpu.make_async_remote_copy(
                out_p.at[chunk, to], got.at[chunk, s], p_send.at[chunk], p_recv.at[chunk],
                device_id=(to, c), device_id_type=MESH,
            ).start()

        got[chunk, pl.ds(s, 1)] = out_p[chunk, pl.ds(s, 1)]

    wait_bytes(flt.at[pl.ds(0, SEQ - 1)], f_recv)
    toeplitz(flt, table)

    for chunk in range(4):
        wait_bytes(got.at[chunk, pl.ds(0, SEQ - 1)], p_recv.at[chunk])
        load_blocks(got, chunk, even, odd)
        for group in range(SEQ // LAGS):
            conv_lags(table, even, odd, acc, chunk, group)

    y = acc[...].reshape(SEQ, SHARE, TOK)
    out_y[...] = jnp.concatenate([y[:, :, :HALF], y[:, :, HALF:]], axis=1).astype(jnp.bfloat16)

    @pl.loop(1, SEQ)
    def _(o):
        to = peer(s, c, o)
        pltpu.make_async_remote_copy(
            out_y.at[to], got_y.at[s], y_send, y_recv, device_id=(to, c), device_id_type=MESH
        ).start()

    got_y[pl.ds(s, 1)] = out_y[pl.ds(s, 1)]
    for part in range(PARTS):
        x_copy(c, part, across, 0).wait_send()
        x_copy(c, part, mate, 1).wait_send()
        x_copy(across, part, mate, 2).wait_send()
    wait_bytes(flt.at[pl.ds(0, SEQ - 1)], f_send)
    for k in range(K):
        wait_bytes(out_p.at[k, pl.ds(0, SEQ - 1)], p_send.at[k])

    wait_bytes(got_y.at[pl.ds(0, SEQ - 1)], y_recv)
    r = got_y[...].astype(jnp.float32)
    for half in range(2):
        block = r[:, half * SHARE : (half + 1) * SHARE, :].reshape(FEAT, HALF)
        o_ref[half * HALF : (half + 1) * HALF, :] = block.T.astype(jnp.bfloat16)
    wait_bytes(out_y.at[pl.ds(0, SEQ - 1)], y_send)


def local(inputs, weights, filters):
    bf16, f32 = jnp.bfloat16, jnp.float32
    vmem = pl.BlockSpec(memory_space=pltpu.VMEM)
    dma = pltpu.SemaphoreType.DMA
    return pl.pallas_call(
        kernel,
        out_shape=jax.ShapeDtypeStruct((TOK, FEAT), bf16),
        in_specs=[vmem, pl.BlockSpec(memory_space=pl.ANY), vmem],
        out_specs=vmem,
        scratch_shapes=[
            pltpu.VMEM((CHAN, TOK, FEAT), bf16),
            pltpu.VMEM((K, CHAN * FEAT, FEAT), bf16),
            pltpu.VMEM((8, HALF), f32),
            pltpu.VMEM((SEQ, 8, HALF), f32),
            pltpu.VMEM((K, TOK, FEAT), f32),
            pltpu.VMEM((K, SEQ, 16, HALF), bf16),
            pltpu.VMEM((K, SEQ, 16, HALF), bf16),
            pltpu.VMEM((K, 2 * SEQ + 1, HALF, HALF), bf16),
            pltpu.VMEM((2, 576, HALF), bf16),
            pltpu.VMEM((2, 592, HALF), bf16),
            pltpu.VMEM((512, TOK), f32),
            pltpu.VMEM((SEQ, 16, HALF), bf16),
            pltpu.VMEM((SEQ, 16, HALF), bf16),
            dma((K,)),
            dma((3, PARTS)),
            dma((3, PARTS)),
            dma,
            dma,
            dma((K,)),
            dma((K,)),
            dma,
            dma,
        ],
        compiler_params=pltpu.CompilerParams(
            collective_id=0, has_side_effects=True, vmem_limit_bytes=56 << 20
        ),
        cost_estimate=pl.CostEstimate(
            flops=11 * 10**9, bytes_accessed=10**7, transcendentals=0
        ),
    )(inputs, weights, filters)


def solution(mesh):
    in_specs = (P("seq", "chan"), P(None, None, "chan"), P(None, "seq"))
    out_specs = P("seq", "chan")
    return jax.shard_map(local, mesh=mesh, in_specs=in_specs, out_specs=out_specs, check_vma=False)
```

time: 87.7 us -> 66.9 us (0.76)
  Pallas kernels: 85.9 us -> 65.1 us
    pallas_call x1, Pallas kernels: 85.9 us -> 65.1 us  [local(): pl.pallas_call(kernel, out_shape=jax.ShapeDtypeStruct((TOK, FEAT), bf16),...]
where the time goes in v1:
time: 66.9 us; the launch traced here: 66.8 us
  Pallas kernels  65.1 us (97%)
  local copies, waits for them, and re-layouts  1.67 us (2%)
    pallas_call x1, Pallas kernels, local(): pl.pallas_call(kernel, out_shape=jax.ShapeDtypeStruct((TOK, FEAT), bf16),...  65.1 us
    unnamed x1, local copies, waits for them, and re-layouts  1.67 us

profile of v1, /device:TPU:1, one launch (start us, length us, event | category | flops | bytes accessed | tf_op | source)
XLA Modules:
  0.0 66.8 jit_solution(8787957858216080704)
XLA Ops:
  0.0 65.1 %shard_map.37 = bf16[256,512]{1,0:T(8,128)(2,1)} custom-call(bf16[256,512]{1,0:T(8,128)(2,1)} %x_ref.1, bf16[4,2048,512]{2,1,0:T(8,128)(2,1)} %w_hbm.1, f32[4,256]{1,0:T(4,128)} %f_ref.1), custom_call_target="tpu_custom_call" | custom-call | flops 11000000512 | bytes 10000000 | tf_op jit(solution)/shard_map/pallas_call | solution.py:235
  65.1 1.7 %copy.5 = bf16[256,512]{1,0:T(8,128)(2,1)} copy(bf16[256,512]{1,0:T(8,128)(2,1)} %shard_map.37) | data formatting | bytes 524288

commit v2 on v1

--- a/solution.py
+++ b/solution.py
@@ -98,9 +98,9 @@
 
 
 def kernel(
-    x_ref, w_hbm, f_ref, o_ref,
-    xs, w, fsrc, flt, part_p, out_p, got, table, even, odd, acc, out_y, got_y,
-    w_sem, xs_send, xs_recv, f_send, f_recv, p_send, p_recv, y_send, y_recv,
+    x_hbm, w_hbm, f_hbm, got_y,
+    xs, w, fsrc, flt, part_p, out_p, got, table, even, odd, acc, out_y,
+    in_sem, w_sem, xs_send, xs_recv, f_send, f_recv, g_send, g_recv, p_send, p_recv, y_send, y_recv,
 ):
     s, c = lax.axis_index("seq"), lax.axis_index("chan")
     mate = c + 1 - 2 * (c % 2)
@@ -113,17 +113,21 @@
 
     @pl.loop(1, SEQ)
     def _(o):
-        pl.semaphore_signal(bar, inc=1, device_id=(peer(s, c, o), c), device_id_type=MESH)
-
+        pl.semaphore_signal(bar, inc=1, device_id=((s + o) % SEQ, c), device_id_type=MESH)
+
+    x_in = pltpu.make_async_copy(x_hbm, xs.at[c], in_sem.at[0])
+    f_in = pltpu.make_async_copy(f_hbm, fsrc, in_sem.at[1])
+    x_in.start()
+    f_in.start()
     for k in range(K):
         pltpu.make_async_copy(w_hbm.at[k], w.at[k], w_sem.at[k]).start()
-    f = f_ref[...]
-    fsrc[...] = jnp.concatenate([f[:, :HALF], f[:, HALF:]], axis=0)
-    xs[pl.ds(c, 1)] = x_ref[...][None]
-    flt[pl.ds(s, 1)] = fsrc[...][None]
     for kk in range(2):
         even[kk, 0:64, :] = jnp.zeros((64, HALF), jnp.bfloat16)
         odd[kk, 0:64, :] = jnp.zeros((64, HALF), jnp.bfloat16)
+    f_in.wait()
+    f = fsrc[...]
+    flt[pl.ds(s, 1)] = jnp.concatenate([f[:, :HALF], f[:, HALF:]], axis=0)[None]
+    x_in.wait()
     pl.semaphore_wait(bar, SEQ - 1 + CHAN - 1)
 
     rows = TOK // PARTS
@@ -140,11 +144,23 @@
     for part in range(PARTS):
         x_copy(c, part, mate, 1).start()
 
-    @pl.loop(1, SEQ)
-    def _(o):
-        pltpu.make_async_remote_copy(
-            fsrc, flt.at[s], f_send, f_recv, device_id=(peer(s, c, o), c), device_id_type=MESH
-        ).start()
+    line, z = s // 8, s % 8
+
+    def near_copy(i):
+        return pltpu.make_async_remote_copy(
+            flt.at[s], flt.at[s], f_send, f_recv,
+            device_id=(line * 8 + (z + i) % 8, c), device_id_type=MESH,
+        )
+
+    def line_copy(i):
+        block = flt.at[pl.ds(line * 8, 8)]
+        return pltpu.make_async_remote_copy(
+            block, block, g_send, g_recv,
+            device_id=((line + i) % 8 * 8 + z, c), device_id_type=MESH,
+        )
+
+    for i in range(1, 8):
+        near_copy(i).start()
 
     def pass_on(part):
         x_copy(across, part, across, 0).wait_recv()
@@ -157,30 +173,41 @@
             preferred_element_type=jnp.float32,
         )
 
-    for k in range(K):
+    def own(k):
         pltpu.make_async_copy(w_hbm.at[k], w.at[k], w_sem.at[k]).wait()
         part_p[k] = project(c, k, 0, TOK)
-    pass_on(0)
+
+    own(0)
+    own(1)
+    wait_bytes(flt.at[pl.ds(0, 7)], f_recv)
+    for i in range(1, 8):
+        line_copy(i).start()
     for part in range(PARTS):
         x_copy(mate, part, mate, 1).wait_recv()
+    part_p[0] += project(mate, 0, 0, TOK)
+    part_p[1] += project(mate, 1, 0, TOK)
+    pass_on(0)
+    own(2)
     pass_on(1)
-    for k in range(K):
-        part_p[k] += project(mate, k, 0, TOK)
+    own(3)
+    part_p[2] += project(mate, 2, 0, TOK)
+    part_p[3] += project(mate, 3, 0, TOK)
 
     for chunk in range(4):
         half, pair = chunk // 2, chunk % 2
-        if chunk == 1:
-            pass_on(2)
-            pass_on(3)
         if pair == 0:
             x_copy(diag, 2 * half, mate, 2).wait_recv()
             x_copy(diag, 2 * half + 1, mate, 2).wait_recv()
+        if chunk == 0:
+            pass_on(2)
         low, high = half * HALF, (half + 1) * HALF
         turned = []
         for k in (2 * pair, 2 * pair + 1):
             p = part_p[k, low:high, :] + project(across, k, low, high) + project(diag, k, low, high)
             turned.append(p.T.reshape(SEQ, SHARE, HALF))
         out_p[chunk] = jnp.concatenate(turned, axis=1).astype(jnp.bfloat16)
+        if chunk == 0:
+            pass_on(3)
 
         @pl.loop(1, SEQ)
         def _(o):
@@ -192,7 +219,7 @@
 
         got[chunk, pl.ds(s, 1)] = out_p[chunk, pl.ds(s, 1)]
 
-    wait_bytes(flt.at[pl.ds(0, SEQ - 1)], f_recv)
+    wait_bytes(flt.at[pl.ds(0, SEQ - 8)], g_recv)
     toeplitz(flt, table)
 
     for chunk in range(4):
@@ -200,9 +227,10 @@
         load_blocks(got, chunk, even, odd)
         for group in range(SEQ // LAGS):
             conv_lags(table, even, odd, acc, chunk, group)
-
-    y = acc[...].reshape(SEQ, SHARE, TOK)
-    out_y[...] = jnp.concatenate([y[:, :, :HALF], y[:, :, HALF:]], axis=1).astype(jnp.bfloat16)
+            if chunk == 3:
+                y = acc[64 * group : 64 * (group + 1), :].reshape(LAGS, SHARE, TOK)
+                y = jnp.concatenate([y[:, :, :HALF], y[:, :, HALF:]], axis=1)
+                out_y[LAGS * group : LAGS * (group + 1)] = y.astype(jnp.bfloat16)
 
     @pl.loop(1, SEQ)
     def _(o):
@@ -216,31 +244,35 @@
         x_copy(c, part, across, 0).wait_send()
         x_copy(c, part, mate, 1).wait_send()
         x_copy(across, part, mate, 2).wait_send()
-    wait_bytes(flt.at[pl.ds(0, SEQ - 1)], f_send)
+    wait_bytes(flt.at[pl.ds(0, 7)], f_send)
+    wait_bytes(flt.at[pl.ds(0, SEQ - 8)], g_send)
     for k in range(K):
         wait_bytes(out_p.at[k, pl.ds(0, SEQ - 1)], p_send.at[k])
 
     wait_bytes(got_y.at[pl.ds(0, SEQ - 1)], y_recv)
-    r = got_y[...].astype(jnp.float32)
+    wait_bytes(out_y.at[pl.ds(0, SEQ - 1)], y_send)
+
+
+def turn_back(y_ref, o_ref):
+    r = y_ref[...].astype(jnp.float32)
     for half in range(2):
         block = r[:, half * SHARE : (half + 1) * SHARE, :].reshape(FEAT, HALF)
         o_ref[half * HALF : (half + 1) * HALF, :] = block.T.astype(jnp.bfloat16)
-    wait_bytes(out_y.at[pl.ds(0, SEQ - 1)], y_send)
 
 
 def local(inputs, weights, filters):
     bf16, f32 = jnp.bfloat16, jnp.float32
     vmem = pl.BlockSpec(memory_space=pltpu.VMEM)
     dma = pltpu.SemaphoreType.DMA
-    return pl.pallas_call(
+    y = pl.pallas_call(
         kernel,
-        out_shape=jax.ShapeDtypeStruct((TOK, FEAT), bf16),
-        in_specs=[vmem, pl.BlockSpec(memory_space=pl.ANY), vmem],
+        out_shape=jax.ShapeDtypeStruct((SEQ, 16, HALF), bf16),
+        in_specs=[pl.BlockSpec(memory_space=pl.ANY)] * 3,
         out_specs=vmem,
         scratch_shapes=[
             pltpu.VMEM((CHAN, TOK, FEAT), bf16),
             pltpu.VMEM((K, CHAN * FEAT, FEAT), bf16),
-            pltpu.VMEM((8, HALF), f32),
+            pltpu.VMEM((K, TOK), f32),
             pltpu.VMEM((SEQ, 8, HALF), f32),
             pltpu.VMEM((K, TOK, FEAT), f32),
             pltpu.VMEM((K, SEQ, 16, HALF), bf16),
@@ -250,10 +282,12 @@
             pltpu.VMEM((2, 592, HALF), bf16),
             pltpu.VMEM((512, TOK), f32),
             pltpu.VMEM((SEQ, 16, HALF), bf16),
-            pltpu.VMEM((SEQ, 16, HALF), bf16),
+            dma((2,)),
             dma((K,)),
             dma((3, PARTS)),
             dma((3, PARTS)),
+            dma,
+            dma,
             dma,
             dma,
             dma((K,)),
@@ -268,6 +302,13 @@
             flops=11 * 10**9, bytes_accessed=10**7, transcendentals=0
         ),
     )(inputs, weights, filters)
+    return pl.pallas_call(
+        turn_back,
+        out_shape=jax.ShapeDtypeStruct((TOK, FEAT), bf16),
+        in_specs=[vmem],
+        out_specs=vmem,
+        cost_estimate=pl.CostEstimate(flops=0, bytes_accessed=2**19, transcendentals=0),
+    )(y)
 
 
 def solution(mesh):

time: 66.9 us -> 63.3 us (0.946)
  Pallas kernels: 65.1 us -> 62.7 us
  local copies, waits for them, and re-layouts: 1.67 us -> 0 us
    pallas_call x1 -> x2, Pallas kernels: 65.1 us -> 62.7 us  [the longest x1 60.9 us: local(): pl.pallas_call(kernel, out_shape=jax.ShapeDtypeStruct((SEQ, 16, HALF), bf...]
    unnamed x1 -> x0, local copies, waits for them, and re-layouts: 1.67 us -> none
where the time goes in v2:
time: 63.3 us; the launch traced here: 62.7 us
  Pallas kernels  62.7 us (99%)
    pallas_call x1, Pallas kernels, local(): pl.pallas_call(kernel, out_shape=jax.ShapeDtypeStruct((SEQ, 16, HALF), bf...  60.9 us
    pallas_call x1, Pallas kernels, local(): pl.pallas_call(turn_back, out_shape=jax.ShapeDtypeStruct((TOK, FEAT), bf1...  1.79 us

profile of v2, /device:TPU:1, one launch (start us, length us, event | category | flops | bytes accessed | tf_op | source)
XLA Modules:
  0.0 62.7 jit_solution(11681967092018704307)
XLA Ops:
  0.0 60.9 %shard_map.37.y_ref = bf16[64,16,128]{2,1,0:T(8,128)(2,1)} custom-call(bf16[256,512]{1,0:T(8,128)(2,1)} %x_hbm.1, bf16[4,2048,512]{2,1,0:T(8,128)(2,1)} %w_hbm.1, f32[4,256]{1,0:T(4,128)} %f_hbm.1), custom_call_target="tpu_custom_call" | custom-call | flops 11000000512 | bytes 10000000 | tf_op jit(solution)/shard_map/pallas_call | solution.py:267
  61.0 1.8 %shard_map.38 = bf16[256,512]{1,0:T(8,128)(2,1)} custom-call(bf16[64,16,128]{2,1,0:T(8,128)(2,1)} %shard_map.37.y_ref), custom_call_target="tpu_custom_call" | custom-call | bytes 524288 | tf_op jit(solution)/shard_map/pallas_call | solution.py:305

commit v3 on v2

--- a/solution.py
+++ b/solution.py
@@ -20,13 +20,22 @@
 PARTS = 4
 
 
-def peer(s, c, o):
-    i, r = (SEQ - o) // 8, (SEQ - o) % 8
-    h = (i + 1) // 2
-    oz = h + (1 - i % 2) * (8 - 2 * h)
-    oz = oz + (c % 2) * (8 - 2 * oz)
+def for_peers(s, c, send):
     yh, x, z = s // 32, (s // 8) % 4, s % 8
-    return ((yh + r // 4) % 2) * 32 + ((x + r) % 4) * 8 + (z + oz) % 8
+    lines = [((yh + r // 4) % 2) * 32 + ((x + r) % 4) * 8 for r in range(8)]
+
+    @pl.loop(0, 7)
+    def _(j):
+        i = 7 - j
+        h = (i + 1) // 2
+        oz = h + (1 - i % 2) * (8 - 2 * h)
+        oz = oz + (c % 2) * (8 - 2 * oz)
+        far = (z + oz) % 8
+        for line in lines:
+            send(line + far)
+
+    for line in lines[1:]:
+        send(line + z)
 
 
 def wait_bytes(ref, sem):
@@ -111,9 +120,9 @@
     for i in range(1, CHAN):
         pl.semaphore_signal(bar, inc=1, device_id=(s, (c + i) % CHAN), device_id_type=MESH)
 
-    @pl.loop(1, SEQ)
-    def _(o):
-        pl.semaphore_signal(bar, inc=1, device_id=((s + o) % SEQ, c), device_id_type=MESH)
+    for_peers(
+        s, c, lambda to: pl.semaphore_signal(bar, inc=1, device_id=(to, c), device_id_type=MESH)
+    )
 
     x_in = pltpu.make_async_copy(x_hbm, xs.at[c], in_sem.at[0])
     f_in = pltpu.make_async_copy(f_hbm, fsrc, in_sem.at[1])
@@ -209,14 +218,13 @@
         if chunk == 0:
             pass_on(3)
 
-        @pl.loop(1, SEQ)
-        def _(o):
-            to = peer(s, c, o)
+        def send_p(to):
             pltpu.make_async_remote_copy(
                 out_p.at[chunk, to], got.at[chunk, s], p_send.at[chunk], p_recv.at[chunk],
                 device_id=(to, c), device_id_type=MESH,
             ).start()
 
+        for_peers(s, c, send_p)
         got[chunk, pl.ds(s, 1)] = out_p[chunk, pl.ds(s, 1)]
 
     wait_bytes(flt.at[pl.ds(0, SEQ - 8)], g_recv)
@@ -232,13 +240,12 @@
                 y = jnp.concatenate([y[:, :, :HALF], y[:, :, HALF:]], axis=1)
                 out_y[LAGS * group : LAGS * (group + 1)] = y.astype(jnp.bfloat16)
 
-    @pl.loop(1, SEQ)
-    def _(o):
-        to = peer(s, c, o)
+    def send_y(to):
         pltpu.make_async_remote_copy(
             out_y.at[to], got_y.at[s], y_send, y_recv, device_id=(to, c), device_id_type=MESH
         ).start()
 
+    for_peers(s, c, send_y)
     got_y[pl.ds(s, 1)] = out_y[pl.ds(s, 1)]
     for part in range(PARTS):
         x_copy(c, part, across, 0).wait_send()

time: 63.3 us -> 63.1 us (level)
  no operation moved by 1% of the time
where the time goes in v3:
time: 63.1 us; the launch traced here: 62.6 us
  Pallas kernels  62.6 us (99%)
    pallas_call x1, Pallas kernels, local(): pl.pallas_call(kernel, out_shape=jax.ShapeDtypeStruct((SEQ, 16, HALF), bf...  60.8 us
    pallas_call x1, Pallas kernels, local(): pl.pallas_call(turn_back, out_shape=jax.ShapeDtypeStruct((TOK, FEAT), bf1...  1.79 us

profile of v3, /device:TPU:1, one launch (start us, length us, event | category | flops | bytes accessed | tf_op | source)
XLA Modules:
  0.0 62.6 jit_solution(6535600057094799173)
XLA Ops:
  0.0 60.8 %shard_map.37.y_ref = bf16[64,16,128]{2,1,0:T(8,128)(2,1)} custom-call(bf16[256,512]{1,0:T(8,128)(2,1)} %x_hbm.1, bf16[4,2048,512]{2,1,0:T(8,128)(2,1)} %w_hbm.1, f32[4,256]{1,0:T(4,128)} %f_hbm.1), custom_call_target="tpu_custom_call" | custom-call | flops 11000000512 | bytes 10000000 | tf_op jit(solution)/shard_map/pallas_call | solution.py:274
  60.8 1.8 %shard_map.38 = bf16[256,512]{1,0:T(8,128)(2,1)} custom-call(bf16[64,16,128]{2,1,0:T(8,128)(2,1)} %shard_map.37.y_ref), custom_call_target="tpu_custom_call" | custom-call | bytes 524288 | tf_op jit(solution)/shard_map/pallas_call | solution.py:312

commit v4 on v2

--- a/solution.py
+++ b/solution.py
@@ -209,13 +209,17 @@
         if chunk == 0:
             pass_on(3)
 
-        @pl.loop(1, SEQ)
-        def _(o):
-            to = peer(s, c, o)
-            pltpu.make_async_remote_copy(
-                out_p.at[chunk, to], got.at[chunk, s], p_send.at[chunk], p_recv.at[chunk],
-                device_id=(to, c), device_id_type=MESH,
-            ).start()
+        if chunk > 0:
+            first, count = (0, 2) if chunk == 1 else (chunk, 1)
+
+            @pl.loop(1, SEQ)
+            def _(o):
+                to = peer(s, c, o)
+                pltpu.make_async_remote_copy(
+                    out_p.at[pl.ds(first, count), to], got.at[pl.ds(first, count), s],
+                    p_send.at[chunk], p_recv.at[chunk],
+                    device_id=(to, c), device_id_type=MESH,
+                ).start()
 
         got[chunk, pl.ds(s, 1)] = out_p[chunk, pl.ds(s, 1)]
 
@@ -223,7 +227,10 @@
     toeplitz(flt, table)
 
     for chunk in range(4):
-        wait_bytes(got.at[chunk, pl.ds(0, SEQ - 1)], p_recv.at[chunk])
+        if chunk == 0:
+            wait_bytes(got.at[pl.ds(0, 2), pl.ds(0, SEQ - 1)], p_recv.at[1])
+        if chunk > 1:
+            wait_bytes(got.at[chunk, pl.ds(0, SEQ - 1)], p_recv.at[chunk])
         load_blocks(got, chunk, even, odd)
         for group in range(SEQ // LAGS):
             conv_lags(table, even, odd, acc, chunk, group)
@@ -246,7 +253,8 @@
         x_copy(across, part, mate, 2).wait_send()
     wait_bytes(flt.at[pl.ds(0, 7)], f_send)
     wait_bytes(flt.at[pl.ds(0, SEQ - 8)], g_send)
-    for k in range(K):
+    wait_bytes(out_p.at[pl.ds(0, 2), pl.ds(0, SEQ - 1)], p_send.at[1])
+    for k in range(2, K):
         wait_bytes(out_p.at[k, pl.ds(0, SEQ - 1)], p_send.at[k])
 
     wait_bytes(got_y.at[pl.ds(0, SEQ - 1)], y_recv)

time: 63.3 us -> 63.6 us (level)
  Pallas kernels: 62.7 us -> 63.5 us
    pallas_call x1, Pallas kernels: 60.9 us -> 61.7 us  [local(): pl.pallas_call(kernel, out_shape=jax.ShapeDtypeStruct((SEQ, 16, HALF), bf...]
where the time goes in v4:
time: 63.6 us; the launch traced here: 63.5 us
  Pallas kernels  63.5 us (100%)
    pallas_call x1, Pallas kernels, local(): pl.pallas_call(kernel, out_shape=jax.ShapeDtypeStruct((SEQ, 16, HALF), bf...  61.7 us
    pallas_call x1, Pallas kernels, local(): pl.pallas_call(turn_back, out_shape=jax.ShapeDtypeStruct((TOK, FEAT), bf1...  1.79 us

profile of v4, /device:TPU:1, one launch (start us, length us, event | category | flops | bytes accessed | tf_op | source)
XLA Modules:
  0.0 63.5 jit_solution(4329448735449354118)
XLA Ops:
  0.0 61.7 %shard_map.37.y_ref = bf16[64,16,128]{2,1,0:T(8,128)(2,1)} custom-call(bf16[256,512]{1,0:T(8,128)(2,1)} %x_hbm.1, bf16[4,2048,512]{2,1,0:T(8,128)(2,1)} %w_hbm.1, f32[4,256]{1,0:T(4,128)} %f_hbm.1), custom_call_target="tpu_custom_call" | custom-call | flops 11000000512 | bytes 10000000 | tf_op jit(solution)/shard_map/pallas_call | solution.py:275
  61.7 1.8 %shard_map.38 = bf16[256,512]{1,0:T(8,128)(2,1)} custom-call(bf16[64,16,128]{2,1,0:T(8,128)(2,1)} %shard_map.37.y_ref), custom_call_target="tpu_custom_call" | custom-call | bytes 524288 | tf_op jit(solution)/shard_map/pallas_call | solution.py:313
